TPU v7x, 256 devices: a whole 4x4x8 slice. The times are simulated.
256 devices in a mesh: dp: 16 (over z, core), rank: 16 (over x, y).
Axes of the slice: x: 4, y: 4, z: 8, core: 2. Of those that a mesh axis runs over, the one named last changes fastest.
Arguments:
- grad_parts: bfloat16 [16, 4096, 14336], P('dp', None, 'rank'), may hold values from -3 to 3
- old_basis: bfloat16 [4096, 512], P('dp'), may hold values from -0.09375 to 0.09375
- moment_one: float32 [512, 14336], P('dp', 'rank'), may hold values from -6 to 6
- moment_two: float32 [512, 14336], P('dp', 'rank'), may hold values from 0.5 to 4
Outputs:
- new_basis: bfloat16 [4096, 512], P('dp')
- moment_new: float32 [512, 14336], P('dp', 'rank')
- second_new: float32 [512, 14336], P('dp', 'rank')
- weight_step: bfloat16 [4096, 14336], P('dp', 'rank')
All inputs are finite; a program needn't handle non-finite values.
Results may differ from a plain program's by a relative error of at most 0.023.
Values may be sent and summed in bfloat16 or wider, within the bound.
No kernel may reach another device: no remote copies, remote signals or barrier semaphores. Data moves between devices by JAX's collectives and lax.ppermute only.
A program may use at most 64 MiB of HBM per device.

v0:
```python
import jax
import jax.numpy as jnp
from jax import lax
from jax.sharding import PartitionSpec as P

highest = lax.Precision.HIGHEST
beta_one = 0.9
beta_two = 0.95
eps = 1e-08


def contract_rows(left_matrix, right_matrix):
    return lax.dot_general(
        left_matrix,
        right_matrix,
        (((0,), (0,)), ((), ())),
        precision=highest,
        preferred_element_type=jnp.float32,
    )


def matmul_high(left_matrix, right_matrix):
    return jnp.dot(left_matrix, right_matrix, precision=highest, preferred_element_type=jnp.float32)


def on_device(grad_parts, old_basis, moment_one, moment_two):
    local_parts = grad_parts[0]
    share_rows = moment_one.shape[0]
    hidden_share = local_parts.shape[1]
    basis_old = old_basis.astype(jnp.float32)
    own_start = lax.axis_index("dp") * share_rows
    gradient = lax.psum_scatter(
        local_parts.astype(jnp.float32).astype(jnp.bfloat16), "dp", scatter_dimension=0, tiled=True
    ).astype(jnp.float32)
    image_part = contract_rows(gradient, basis_old)
    images = lax.psum(image_part, "dp")
    sketch_part = matmul_high(gradient, images)
    sketch = lax.psum(sketch_part, "rank")
    gram_part = contract_rows(sketch, sketch)
    gram_matrix = lax.psum(gram_part, "dp")
    factor = jnp.linalg.cholesky(gram_matrix)
    basis_exact = jax.scipy.linalg.solve_triangular(factor, sketch.T, lower=True).T
    rotation = lax.psum(contract_rows(basis_exact, basis_old), "dp")
    new_basis = basis_exact.astype(jnp.bfloat16)
    columns = new_basis.astype(jnp.float32)
    projected = lax.psum_scatter(
        contract_rows(columns, gradient), "dp", scatter_dimension=0, tiled=True
    )
    rotation_block = lax.dynamic_slice(
        rotation, (0, own_start), (share_rows * lax.axis_size("dp"), share_rows)
    )
    stacked_terms = lax.psum_scatter(
        jnp.concatenate(
            [
                matmul_high(rotation_block, moment_one),
                matmul_high(rotation_block * rotation_block, moment_two),
            ],
            axis=1,
        ),
        "dp",
        scatter_dimension=0,
        tiled=True,
    )
    first_rotated = stacked_terms[:, :hidden_share]
    second_rotated = stacked_terms[:, hidden_share:]
    moment_new = beta_one * first_rotated + (1.0 - beta_one) * projected
    second_new = beta_two * second_rotated + (1.0 - beta_two) * projected * projected
    adam_update = (moment_new / (jnp.sqrt(second_new) + eps)).astype(jnp.bfloat16)
    columns = new_basis
    weight_step = jnp.dot(
        columns,
        lax.all_gather(adam_update, "dp", axis=0, tiled=True),
        preferred_element_type=jnp.float32,
    ).astype(jnp.bfloat16)
    return (new_basis, moment_new, second_new, weight_step)


def solution(mesh):
    in_specs = (P("dp", None, "rank"), P("dp", None), P("dp", "rank"), P("dp", "rank"))
    out_specs = (P("dp", None), P("dp", "rank"), P("dp", "rank"), P("dp", "rank"))
    return jax.shard_map(
        on_device, mesh=mesh, in_specs=in_specs, out_specs=out_specs, check_vma=False
    )
```

profile of v0, /device:TPU:1, one launch (start us, length us, event | category | flops | bytes accessed | tf_op | source)
XLA Modules:
  0.0 825.0 jit_solution(4705651888625342255)
XLA Ops:
  7.2 0.7 reduce-scatter.4.cloned.1.call-update
  8.0 72.1 %reduce-scatter.4.cloned.1.call-done = bf16[256,896]{1,0:T(8,128)(2,1)} async-done(((bf16[4096,896]{1,0:T(8,128)(2,1)}), bf16[256,896]{1,0:T(8,128)(2,1)}) %reduce-scatter.4.cloned.1.call-update) | async-done | bytes 458768 | tf_op jit(solution)/shard_map/reduce_scatter | solution.py:32
  80.1 2.7 fusion.49
  82.9 115.5 %all-reduce.6.cloned.1.call-done = f32[896,512]{1,0:T(8,128)} async-done(((f32[896,512]{1,0:T(8,128)}), f32[896,512]{1,0:T(8,128)}) %all-reduce.6.cloned.1.call-update) | async-done | bytes 1835024 | tf_op jit(solution)/shard_map/psum | solution.py:36
  198.4 3.9 convolution_bitcast_fusion
  202.4 94.5 %all-reduce.8.cloned.1.call-done = f32[256,512]{0,1:T(8,128)} async-done(((f32[256,512]{0,1:T(8,128)}), f32[256,512]{0,1:T(8,128)}) %all-reduce.8.cloned.1.call-update) | async-done | bytes 524304 | tf_op jit(solution)/shard_map/psum | solution.py:38
  296.9 3.3 fusion.50
  300.8 111.7 %all-reduce.10.cloned.1.call-done = f32[512,512]{0,1:T(8,128)} async-done(((f32[512,512]{0,1:T(8,128)}), f32[512,512]{0,1:T(8,128)}) %all-reduce.10.cloned.1.call-update) | async-done | bytes 1048592 | tf_op jit(solution)/shard_map/psum | solution.py:40
  412.5 1.6 copy.9
  414.4 1.0 copy-done.4
  415.4 11.7 %cholesky.104 = f32[128,128]{1,0:T(8,128)S(1)} custom-call(f32[128,128]{1,0:T(8,128)S(1)} %cholesky.266), custom_call_target="Cholesky" | custom-call | tf_op jit(solution)/shard_map/jit(cholesky)/cholesky | solution.py:41
  427.1 9.8 %custom-call.31 = f32[1,128,128]{1,2,0:T(8,128)S(1)} custom-call(f32[1,128,128]{2,1,0:T(8,128)S(1)} %get-tuple-element.38), custom_call_target="InvertDiagBlocksLowerTriangular" | custom-call | tf_op jit(solution)/shard_map/jit(cholesky)/cholesky | solution.py:41
  437.1 1.2 constant_dynamic-update-slice_fusion.3
  438.3 1.3 convolution_subtract_fusion
  439.6 11.7 %cholesky.217 = f32[128,128]{1,0:T(8,128)S(1)} custom-call(f32[128,128]{1,0:T(8,128)S(1)} %cholesky.270), custom_call_target="Cholesky" | custom-call | tf_op jit(solution)/shard_map/jit(cholesky)/cholesky | solution.py:41
  451.3 10.0 %custom-call.32 = f32[1,128,128]{1,2,0:T(8,128)S(1)} custom-call(f32[1,128,128]{2,1,0:T(8,128)S(1)} %get-tuple-element.35), custom_call_target="InvertDiagBlocksLowerTriangular" | custom-call | tf_op jit(solution)/shard_map/jit(cholesky)/cholesky | solution.py:41
  461.6 1.3 convolution_subtract_fusion.3
  462.9 11.7 %cholesky.238 = f32[128,128]{1,0:T(8,128)S(1)} custom-call(f32[128,128]{1,0:T(8,128)S(1)} %cholesky.275), custom_call_target="Cholesky" | custom-call | tf_op jit(solution)/shard_map/jit(cholesky)/cholesky | solution.py:41
  474.6 0.6 compare_reduce_fusion.1
  475.3 9.8 %custom-call.33 = f32[1,128,128]{1,2,0:T(8,128)S(1)} custom-call(f32[1,128,128]{2,1,0:T(8,128)S(1)} %get-tuple-element.32), custom_call_target="InvertDiagBlocksLowerTriangular" | custom-call | tf_op jit(solution)/shard_map/jit(cholesky)/cholesky | solution.py:41
  485.3 1.2 convolution_subtract_fusion.5
  486.5 11.7 %cholesky.255 = f32[128,128]{1,0:T(8,128)S(1)} custom-call(f32[128,128]{1,0:T(8,128)S(1)} %convolution_subtract_fusion.5), custom_call_target="Cholesky" | custom-call | tf_op jit(solution)/shard_map/jit(cholesky)/cholesky | solution.py:41
  498.3 0.7 compare_reduce_fusion
  499.0 0.6 compare_reduce_fusion.2
  502.3 1.3 select_select_fusion
  503.6 11.6 %while.1 = (s32[]{:T(128)}, f32[512,512]{1,0:T(8,128)}, s32[4,2]{0,1:T(2,128)S(1)}, f32[4,128,128]{2,1,0:T(8,128)S(1)}, s32[]{:T(128)}) while((s32[]{:T(128)}, f32[512,512]{1,0:T(8,128)}, s32[4,2]{0,1:T(2,128)S(1)}, f32[4,128,128]{2,1,0:T(8,128)S(1)}, s32[]{:T(128)}) %tuple.34), condition=%wide.while_cond, body=%wide.while_body.sunk | while | flops 2 | bytes 131189 | solution.py:42
  504.2 2.3 bitcast_dynamic-update-slice_fusion.2
  506.6 0.5 fusion.68
  507.1 2.3 bitcast_dynamic-update-slice_fusion.2
  510.0 2.3 bitcast_dynamic-update-slice_fusion.2
  512.4 0.5 fusion.68
  512.9 2.2 bitcast_dynamic-update-slice_fusion.2
  515.1 39.3 %custom-call.34 = f32[4,128,128]{1,2,0:T(8,128)S(1)} custom-call(f32[4,128,128]{2,1,0:T(8,128)S(1)} %get-tuple-element.11), custom_call_target="InvertDiagBlocksLowerTriangular" | custom-call | tf_op jit(solution)/shard_map/jit(_solve_triangular)/triangular_solve | solution.py:42
  554.8 1.1 convolution_subtract_fusion.4
  556.2 1.2 convolution_subtract_fusion.2
  557.7 1.3 convolution_subtract_fusion.1
  559.4 1.7 fusion.6
  561.2 1.7 fusion.43
  562.9 109.9 %all-reduce.12.cloned.1.call-done = f32[512,512]{0,1:T(8,128)} async-done(((f32[512,512]{0,1:T(8,128)}), f32[512,512]{0,1:T(8,128)}) %all-reduce.12.cloned.1.call-update) | async-done | bytes 1048592 | tf_op jit(solution)/shard_map/psum | solution.py:43
  672.8 2.5 fusion.32
  675.3 2.5 fusion.35
  677.8 2.1 pad_maximum_fusion
  679.9 0.8 copy.10
  680.8 50.5 %reduce-scatter.8.cloned.1.call-done = f32[32,896]{1,0:T(8,128)} async-done(((f32[512,896]{1,0:T(8,128)}), f32[32,896]{1,0:T(8,128)}) %reduce-scatter.8.cloned.1.call-update) | async-done | bytes 114704 | tf_op jit(solution)/shard_map/reduce_scatter | solution.py:46
  731.3 63.0 %reduce-scatter.6.cloned.1.call-done = f32[32,1792]{1,0:T(8,128)} async-done(((f32[512,1792]{1,0:T(8,128)}), f32[32,1792]{1,0:T(8,128)}) %reduce-scatter.6.cloned.1.call-update) | async-done | bytes 229392 | tf_op jit(solution)/shard_map/reduce_scatter | solution.py:52
  794.3 1.8 divide_convert_fusion
  796.1 20.6 %all_gather.3 = bf16[512,896]{1,0:T(8,128)(2,1)S(1)} all-gather(bf16[32,896]{1,0:T(8,128)(2,1)S(1)} %get-tuple-element.24), channel_id=1, replica_groups=mesh['dp'=16,'rank'=16] {'dp'}, dimensions={0}, use_global_device_ids=true | all-gather | bytes 974848 | tf_op jit(solution)/shard_map/all_gather | solution.py:72
  816.7 1.2 convolution_convert_fusion
  (51 shorter events, 4.5 us)
Async XLA Ops:
  7.2 72.9 %copy-start = (bf16[256,512]{1,0:T(8,128)(2,1)S(1)}, bf16[256,512]{1,0:T(8,128)(2,1)}, u32[]{:S(2)}) copy-start(bf16[256,512]{1,0:T(8,128)(2,1)} %param.5) | copy-start | bytes 786436
  7.2 72.9 %reduce-scatter.4.cloned.1.call-start = ((), (), s32[]{:S(2)}) async-start(), calls=%async_computation.3 | async-start | bytes 7798784 | tf_op jit(solution)/shard_map/reduce_scatter | solution.py:32
  7.9 190.5 %all-reduce.6.cloned.1.call-start = ((), (), s32[]{:S(2)}) async-start(), calls=%async_computation.4 | async-start | bytes 3670016 | tf_op jit(solution)/shard_map/psum | solution.py:36
  80.1 118.3 %copy-start.3 = (bf16[256,896]{1,0:T(8,128)(2,1)S(1)}, bf16[256,896]{1,0:T(8,128)(2,1)}, u32[]{:S(2)}) copy-start(bf16[256,896]{1,0:T(8,128)(2,1)} %reduce-scatter.4.cloned.1.call-done) | copy-start | bytes 1376260
  82.8 214.1 %all-reduce.8.cloned.1.call-start = ((), (), s32[]{:S(2)}) async-start(), calls=%async_computation.5 | async-start | bytes 1048576 | tf_op jit(solution)/shard_map/psum | solution.py:38
  202.4 210.1 %all-reduce.10.cloned.1.call-start = ((), (), s32[]{:S(2)}) async-start(), calls=%async_computation.6 | async-start | bytes 2097152 | tf_op jit(solution)/shard_map/psum | solution.py:40
  300.2 372.6 %all-reduce.12.cloned.1.call-start = ((), (), s32[]{:S(2)}) async-start(), calls=%async_computation.7 | async-start | bytes 2097152 | tf_op jit(solution)/shard_map/psum | solution.py:43
  412.5 1.7 copy-start.2
  414.4 1.0 copy-start.4
  474.6 79.8 %copy-start.1 = (f32[256,512]{0,1:T(8,128)S(1)}, f32[256,512]{0,1:T(8,128)}, u32[]{:S(2)}) copy-start(f32[256,512]{0,1:T(8,128)} %all-reduce.8.cloned.1.call-done) | copy-start | bytes 1572868
  561.1 111.7 %copy-start.5 = (f32[32,896]{1,0:T(8,128)S(1)}, f32[32,896]{1,0:T(8,128)}, u32[]{:S(2)}) copy-start(f32[32,896]{1,0:T(8,128)} %param.7) | copy-start | bytes 344068
  561.1 170.2 %reduce-scatter.8.cloned.1.call-start = ((), (), s32[]{:S(2)}) async-start(), calls=%async_computation.9 | async-start | bytes 1949696 | tf_op jit(solution)/shard_map/reduce_scatter | solution.py:46
  562.8 112.5 %copy-start.6 = (f32[32,896]{1,0:T(8,128)S(1)}, f32[32,896]{1,0:T(8,128)}, u32[]{:S(2)}) copy-start(f32[32,896]{1,0:T(8,128)} %param.6) | copy-start | bytes 344068
  562.9 231.5 %reduce-scatter.6.cloned.1.call-start = ((), (), s32[]{:S(2)}) async-start(), calls=%async_computation.8 | async-start | bytes 3899392 | tf_op jit(solution)/shard_map/reduce_scatter | solution.py:52
Sparse Core Ops, SparseCore 0:
  10.6 69.4 reduce-scatter.3
  83.0 115.3 all-reduce.5
  202.5 94.4 all-reduce.7
  300.3 112.0 all-reduce.9
  561.2 111.5 all-reduce.11
  675.2 56.0 reduce-scatter.7
  734.1 60.2 reduce-scatter.5
where the time goes:
time: 829 us; the launch traced here: 825 us
  waiting for transfers between devices  618 us (75%)
  other arithmetic  123 us (15%)
  matrix products  29.8 us (4%)
  blocking collectives  20.6 us (2%)
  between operations  17.3 us (2%)
  local copies, waits for them, and re-layouts  15.1 us (2%)
    psum x1, waiting for transfers between devices, on_device(): images = lax.psum(image_part, 'dp')  116 us
    psum x1, waiting for transfers between devices, on_device(): gram_matrix = lax.psum(gram_part, 'dp')  112 us
    psum x1, waiting for transfers between devices, on_device(): rotation = lax.psum(contract_rows(basis_exact, basis_old), 'dp')  110 us
    psum x1, waiting for transfers between devices, on_device(): sketch = lax.psum(sketch_part, 'rank')  94.5 us
    another operation x14, other arithmetic, on_device(): factor = jnp.linalg.cholesky(gram_matrix)  78.6 us
    reduce_scatter x1, waiting for transfers between devices, on_device(): lax.psum_scatter(local_parts.astype(jnp.float32).astype(jnp.bfloat16), 'd...  72.1 us
    reduce_scatter x1, waiting for transfers between devices, on_device(): lax.psum_scatter(jnp.concatenate([matmul_high(rotation_block, moment_one)...  63 us
    reduce_scatter x1, waiting for transfers between devices, on_device(): lax.psum_scatter(contract_rows(columns, gradient), 'dp', scatter_dimensio...  50.5 us
  transfers between devices with their start and end apart: 7, of which 7 were waited for; matrix products, arithmetic and copies ran while one was open for 1% of the time, Pallas kernels for 0%

commit v1 on v0

v1 whole, which is shorter than its diff:
```python
import jax
import jax.numpy as jnp
from jax import lax
from jax.experimental import pallas as pl
from jax.experimental.pallas import tpu as pltpu
from jax.sharding import PartitionSpec as P

highest = lax.Precision.HIGHEST
beta_one = 0.9
beta_two = 0.95
eps = 1e-08
bf16 = jnp.bfloat16
f32 = jnp.float32
block_size = 128
group_size = 8

n_z = 8
n_side = 4
swap_cores = [(z * 2 + c, z * 2 + 1 - c) for z in range(n_z) for c in range(2)]
z_groups = [[z * 2 + c for z in range(n_z)] for c in range(2)]


def z_shift(step):
    return [(z * 2 + c, ((z + step) % n_z) * 2 + c) for z in range(n_z) for c in range(2)]


def x_shift(step):
    return [
        (x * n_side + y, ((x + step) % n_side) * n_side + y)
        for x in range(n_side)
        for y in range(n_side)
    ]


def y_shift(step):
    return [
        (x * n_side + y, x * n_side + (y + step) % n_side)
        for x in range(n_side)
        for y in range(n_side)
    ]


def dot_exact(left, right, dims):
    return lax.dot_general(
        left, right, (dims, ((), ())), precision=highest, preferred_element_type=f32
    )


def dot_fast(left, right, dims):
    return lax.dot_general(left, right, (dims, ((), ())), preferred_element_type=f32)


def identity(n):
    return (
        lax.broadcasted_iota(jnp.int32, (n, n), 0) == lax.broadcasted_iota(jnp.int32, (n, n), 1)
    ).astype(f32)


def inverse_of_block_factor(block):
    n = block_size
    left = block
    right = identity(n)
    finished = []
    for group in range(n // group_size):
        rows = n - group * group_size
        row_index = lax.broadcasted_iota(jnp.int32, (rows, n), 0)
        columns = []
        for j in range(group_size):
            at = group * group_size + j
            columns.append(jnp.broadcast_to(left[:, at : at + 1], (rows, n)))
        scales = []
        for j in range(group_size):
            pivot = columns[j][j : j + 1, :]
            multiplier = jnp.where(row_index > j, columns[j] * (1.0 / pivot), 0.0)
            scales.append(lax.rsqrt(pivot))
            for k in range(j + 1, group_size):
                columns[k] = columns[k] - multiplier * columns[k][j : j + 1, :]
            if group < n // group_size - 1:
                left = left - multiplier * left[j : j + 1, :]
            right = right - multiplier * right[j : j + 1, :]
        finished.append(right[:group_size, :] * jnp.concatenate(scales, axis=0))
        left = left[group_size:, :]
        right = right[group_size:, :]
    return jnp.concatenate(finished, axis=0)


def factor_kernel(gram_ref, inverse_ref, work):
    n = gram_ref.shape[0]
    work[...] = gram_ref[...]
    inverse_ref[...] = identity(n)
    for k in range(n // block_size):
        low = k * block_size
        high = low + block_size
        diagonal = inverse_of_block_factor(work[low:high, low:high])
        inverse_rows = dot_exact(diagonal, inverse_ref[low:high, :high], ((1,), (0,)))
        inverse_ref[low:high, :high] = inverse_rows
        if high < n:
            factor_rows = dot_exact(diagonal, work[low:high, high:], ((1,), (0,)))
            work[high:, high:] = work[high:, high:] - dot_exact(
                factor_rows, factor_rows, ((0,), (0,))
            )
            inverse_ref[high:, :high] = inverse_ref[high:, :high] - dot_exact(
                factor_rows, inverse_rows, ((0,), (0,))
            )


def inverse_factor(gram_matrix):
    n = gram_matrix.shape[0]
    return pl.pallas_call(
        factor_kernel,
        out_shape=jax.ShapeDtypeStruct((n, n), f32),
        scratch_shapes=[pltpu.VMEM((n, n), f32)],
        compiler_params=pltpu.CompilerParams(vmem_limit_bytes=32 * 1024 * 1024),
    )(gram_matrix)


def pick(blocks, index):
    return lax.dynamic_index_in_dim(blocks, index, 0, keepdims=False)


def sum_gradient(local_parts, z, core):
    d_model, hidden = local_parts.shape
    share = hidden // (2 * n_z)
    turned = local_parts.T.reshape(n_z, 2, share, d_model)
    other = lax.ppermute(lax.dynamic_index_in_dim(turned, 1 - core, 1, keepdims=False), "dp", swap_cores)
    keep = lax.dynamic_index_in_dim(turned, core, 1, keepdims=False)
    pair = (keep.astype(f32) + other.astype(f32)).astype(bf16)
    half = d_model // 2
    result = []
    for lanes, hops_up, hops_down in ((slice(0, half), 4, 3), (slice(half, d_model), 3, 4)):
        piece = pair[:, :, lanes]
        total = pick(piece, z).astype(f32)
        for hops, direction in ((hops_up, 1), (hops_down, -1)):
            moving = None
            for hop in range(hops, 0, -1):
                own = pick(piece, (z + direction * hop) % n_z)
                if moving is not None:
                    own = (own.astype(f32) + moving.astype(f32)).astype(bf16)
                moving = lax.ppermute(own, "dp", z_shift(direction))
            total = total + moving.astype(f32)
        result.append(total.astype(bf16))
    return jnp.concatenate(result, axis=1)


def scatter_side(blocks, shift, at):
    total = pick(blocks, at).astype(f32)
    for step in (2, 1, 3):
        arrived = lax.ppermute(pick(blocks, (at + step) % n_side), "rank", shift(step))
        total = total + arrived.astype(f32)
    return total


def gather_side(block, shift, at):
    out = jnp.zeros((n_side,) + block.shape, block.dtype)
    out = lax.dynamic_update_index_in_dim(out, block, at, 0)
    for step in (2, 1, 3):
        arrived = lax.ppermute(block, "rank", shift(step))
        out = lax.dynamic_update_index_in_dim(out, arrived, (at - step) % n_side, 0)
    return out


def on_device(grad_parts, old_basis, moment_one, moment_two):
    local_parts = grad_parts[0]
    d_model, hidden_share = local_parts.shape
    share_rows, rank = moment_one.shape[0], old_basis.shape[1]
    own = lax.axis_index("dp")
    z, core = own // 2, own % 2
    place = lax.axis_index("rank")
    x, y = place // n_side, place % n_side
    n_dp = 2 * n_z
    hidden_own = hidden_share // n_dp

    basis_all = lax.all_gather(old_basis, "dp", axis=0, tiled=True)
    moments = jnp.concatenate([moment_one, moment_two], axis=0).T
    moments = lax.all_to_all(moments, "dp", 0, 0, tiled=True)
    moments = moments.reshape(n_dp, hidden_own, 2, share_rows).transpose(2, 1, 0, 3)
    moments = moments.reshape(2, hidden_own, rank)

    gradient = sum_gradient(local_parts, z, core)
    images = dot_fast(gradient, basis_all, ((1,), (0,)))
    images_high = images.astype(bf16)
    images_low = (images - images_high.astype(f32)).astype(bf16)
    sketch_part = dot_fast(
        jnp.concatenate([gradient, gradient], axis=0),
        jnp.concatenate([images_high, images_low], axis=0),
        ((0,), (0,)),
    ).astype(bf16)

    sketch_part = sketch_part.reshape(2, d_model // 2, rank)
    arrived = lax.ppermute(pick(sketch_part, 1 - core), "dp", swap_cores)
    sketch_part = (pick(sketch_part, core).astype(f32) + arrived.astype(f32)).astype(bf16)
    rows = d_model // 2 // (n_side * n_side) // 2
    sketch_part = sketch_part.reshape(n_side, n_side, 2, rows, rank)
    first = scatter_side(sketch_part[:, :, 0], x_shift, x).astype(bf16)
    second = scatter_side(sketch_part[:, :, 1].swapaxes(0, 1), y_shift, y).astype(bf16)
    first = scatter_side(first, y_shift, y).astype(bf16)
    second = scatter_side(second, x_shift, x).astype(bf16)
    sketch_part = jnp.concatenate([first, second], axis=0)
    sketch_part = lax.all_to_all(
        sketch_part, "dp", 0, 0, tiled=True, axis_index_groups=z_groups
    ).reshape(n_z, 2 * rows // n_z, rank)
    sketch_rows = jnp.sum(sketch_part.astype(f32), axis=0).astype(bf16)

    sketch = lax.all_gather(sketch_rows, "dp", axis=0, tiled=True, axis_index_groups=z_groups)
    first, second = sketch[:rows], sketch[rows:]
    first = gather_side(first, y_shift, y)
    second = gather_side(second, x_shift, x)
    first = gather_side(first, x_shift, x)
    second = gather_side(second, y_shift, y).swapaxes(0, 1)
    sketch = jnp.stack([first, second], axis=2).reshape(d_model // 2, rank)
    arrived = lax.ppermute(sketch, "dp", swap_cores)
    sketch = jnp.where(
        core == 0,
        jnp.concatenate([sketch, arrived], axis=0),
        jnp.concatenate([arrived, sketch], axis=0),
    )

    gram_matrix = dot_fast(sketch, sketch, ((0,), (0,)))
    cosines = dot_fast(sketch, basis_all, ((0,), (0,)))
    factor_inverse = inverse_factor(gram_matrix)
    back_images = dot_fast(gradient, sketch, ((1,), (0,)))

    rotation = dot_exact(factor_inverse, cosines, ((1,), (0,)))
    sketch_own = lax.dynamic_slice_in_dim(
        sketch, own * old_basis.shape[0], old_basis.shape[0], 0
    )
    new_basis = dot_exact(sketch_own.astype(f32), factor_inverse, ((1,), (1,))).astype(bf16)
    projected = dot_exact(back_images, factor_inverse, ((1,), (1,)))
    first_rotated = dot_exact(moments[0], rotation, ((1,), (1,)))
    second_rotated = dot_exact(moments[1], rotation * rotation, ((1,), (1,)))
    moment_new = beta_one * first_rotated + (1.0 - beta_one) * projected
    second_new = beta_two * second_rotated + (1.0 - beta_two) * projected * projected
    adam_update = (moment_new / (jnp.sqrt(second_new) + eps)).astype(bf16)
    adam_all = lax.all_gather(adam_update, "dp", axis=0, tiled=True)
    weight_step = dot_fast(new_basis, adam_all, ((1,), (1,))).astype(bf16)

    back = jnp.stack([moment_new, second_new]).reshape(2, hidden_own, n_dp, share_rows)
    back = back.transpose(2, 1, 0, 3).reshape(n_dp * hidden_own, 2 * share_rows)
    back = lax.all_to_all(back, "dp", 0, 0, tiled=True).T
    return (new_basis, back[:share_rows], back[share_rows:], weight_step)


def solution(mesh):
    in_specs = (P("dp", None, "rank"), P("dp", None), P("dp", "rank"), P("dp", "rank"))
    out_specs = (P("dp", None), P("dp", "rank"), P("dp", "rank"), P("dp", "rank"))
    return jax.shard_map(
        on_device, mesh=mesh, in_specs=in_specs, out_specs=out_specs, check_vma=False
    )
```

time: 829 us -> 329 us (0.40)
  waiting for transfers between devices: 618 us -> 107 us
  other arithmetic: 123 us -> 15.4 us
  starting transfers between devices: 0.75 us -> 90.3 us
  Pallas kernels: 0 us -> 18.9 us
  blocking collectives: 20.6 us -> 35.2 us
  matrix products: 29.8 us -> 17.8 us
  local copies, waits for them, and re-layouts: 15.1 us -> 25.3 us
    psum x4 -> x0, waiting for transfers between devices: 432 us -> none  [the longest x1 116 us: on_device(): images = lax.psum(image_part, 'dp')]
    reduce_scatter x3 -> x0, waiting for transfers between devices: 186 us -> none  [the longest x1 72.1 us: on_device(): lax.psum_scatter(local_parts.astype(jnp.float32).astype(jnp.bfloat16), 'd...]
    another operation x17 -> x1, other arithmetic: 119 us -> 0.2 us  [on_device(): sketch = jnp.stack([first, second], axis=2).reshape(d_model // 2, rank)]
    ppermute x0 -> x41, waiting for transfers between devices: none -> 79.6 us  [the longest x14 54 us: sum_gradient(): moving = lax.ppermute(own, 'dp', z_shift(direction))]
    ppermute x0 -> x41, starting transfers between devices: none -> 77.9 us  [the longest x12 30 us: scatter_side(): lax.ppermute(pick(blocks, (at + step) % n_side), 'rank', shift(step))]
    all_to_all x0 -> x3, waiting for transfers between devices: none -> 27.2 us  [the longest x1 11.1 us: on_device(): moments = lax.all_to_all(moments, 'dp', 0, 0, tiled=True)]
    pallas_call x0 -> x1, Pallas kernels: none -> 18.9 us  [inverse_factor(): pl.pallas_call(factor_kernel, out_shape=jax.ShapeDtypeStruct((n, n), f32)...]
    all_gather x1 -> x2, blocking collectives: 20.6 us -> 35.2 us  [the longest x1 18.2 us: on_device(): lax.all_gather(sketch_rows, 'dp', axis=0, tiled=True, axis_index_groups=z...]
  transfers between devices with their start and end apart: 7 -> 45, of which waited for: 7 -> 24; matrix products, arithmetic and copies ran while one was open for 1% -> 4% of each run, Pallas kernels for 0% -> 0%
where the time goes in v1:
time: 329 us; the launch traced here: 325 us
  waiting for transfers between devices  107 us (33%)
  starting transfers between devices  90.3 us (27%)
  blocking collectives  35.2 us (11%)
  local copies, waits for them, and re-layouts  25.3 us (8%)
  Pallas kernels  18.9 us (6%)
  matrix products  17.8 us (5%)
  other arithmetic  15.4 us (5%)
  between operations  15.1 us (5%)
    ppermute x14, waiting for transfers between devices, sum_gradient(): moving = lax.ppermute(own, 'dp', z_shift(direction))  54 us
    ppermute x12, starting transfers between devices, scatter_side(): lax.ppermute(pick(blocks, (at + step) % n_side), 'rank', shift(step))  30 us
    pallas_call x1, Pallas kernels, inverse_factor(): pl.pallas_call(factor_kernel, out_shape=jax.ShapeDtypeStruct((n, n), f32)...  18.9 us
    all_gather x1, blocking collectives, on_device(): lax.all_gather(sketch_rows, 'dp', axis=0, tiled=True, axis_index_groups=z...  18.2 us
    all_gather x1, blocking collectives, on_device(): adam_all = lax.all_gather(adam_update, 'dp', axis=0, tiled=True)  17 us
    ppermute x14, starting transfers between devices, sum_gradient(): moving = lax.ppermute(own, 'dp', z_shift(direction))  15.4 us
    unnamed x17, local copies, waits for them, and re-layouts  14.9 us
    ppermute x1, starting transfers between devices, on_device(): arrived = lax.ppermute(sketch, 'dp', swap_cores)  14.9 us
  transfers between devices with their start and end apart: 45, of which 24 were waited for; matrix products, arithmetic and copies ran while one was open for 4% of the time, Pallas kernels for 0%

profile of v1, /device:TPU:1, one launch (start us, length us, event | category | flops | bytes accessed | tf_op | source)
XLA Modules:
  0.0 324.8 jit_solution(12285000988581483622)
XLA Ops:
  7.2 10.7 %copy.52 = bf16[1,4096,896]{1,2,0:T(8,128)(2,1)} copy(bf16[1,4096,896]{2,1,0:T(8,128)(2,1)} %param.4) | data formatting | bytes 14680064 | tf_op args[0]
  17.9 4.3 %dynamic-slice_bitcast_fusion = bf16[8,56,4096]{2,1,0:T(8,128)(2,1)} fusion(bf16[8,2,56,4096]{3,2,1,0:T(8,128)(2,1)} %bitcast.188, s32[]{:T(128)S(6)} %select_n.257), kind=kLoop, calls=%fused_computation.6 | loop fusion | bytes 7340036 | tf_op jit(solution)/shard_map/jit(dynamic_index_in_dim)/squeeze | solution.py:125
  22.2 3.2 collective-permute-start
  25.6 6.2 %collective-permute-done = bf16[8,56,4096]{2,1,0:T(8,128)(2,1)} collective-permute-done((bf16[8,56,4096]{2,1,0:T(8,128)(2,1)}, bf16[8,56,4096]{2,1,0:T(8,128)(2,1)}, u32[]{:S(2)}, u32[]{:S(2)}) %collective-permute-start) | collective-permute-done | bytes 3670048 | tf_op jit(solution)/shard_map/ppermute | solution.py:125
  31.8 4.7 %fusion = bf16[8,56,4096]{2,1,0:T(8,128)(2,1)S(1)} fusion(bf16[8,56,4096]{2,1,0:T(8,128)(2,1)} %collective-permute-done, bf16[8,2,56,4096]{3,2,1,0:T(8,128)(2,1)} %bitcast.189, s32[]{:T(128)S(6)} %select_n.256), kind=kLoop, calls=%fused_computation.1 | loop fusion | flops 7340032 | bytes 11010052 | tf_op jit(solution)/shard_map/convert_element_type | solution.py:127
  37.1 3.9 %collective-permute-start.5 = (bf16[56,2048]{1,0:T(8,128)(2,1)S(1)}, bf16[56,2048]{1,0:T(8,128)(2,1)S(1)}, u32[]{:S(2)}, u32[]{:S(2)}) collective-permute-start(bf16[56,2048]{1,0:T(8,128)(2,1)S(1)} %get-tuple-element.13), channel_id=1, source_target_pairs={{0,224},{16,240},{32,0},{48,16},{64,32},{80,48},{96,64},{112,80},{... | collective-permute-start | bytes 688136 | tf_op jit(solution)/shard_map/ppermute | solution.py:139
  41.2 2.7 collective-permute-start.11
  43.8 7.7 %collective-permute-done.1 = bf16[56,2048]{1,0:T(8,128)(2,1)S(1)} collective-permute-done((bf16[56,2048]{1,0:T(8,128)(2,1)S(1)}, bf16[56,2048]{1,0:T(8,128)(2,1)S(1)}, u32[]{:S(2)}, u32[]{:S(2)}) %collective-permute-start.1) | collective-permute-done | bytes 229408 | tf_op jit(solution)/shard_map/ppermute | solution.py:139
  51.7 9.7 %collective-permute-done.8 = bf16[56,2048]{1,0:T(8,128)(2,1)S(1)} collective-permute-done((bf16[56,2048]{1,0:T(8,128)(2,1)S(1)}, bf16[56,2048]{1,0:T(8,128)(2,1)S(1)}, u32[]{:S(2)}, u32[]{:S(2)}) %collective-permute-start.8) | collective-permute-done | bytes 229408 | tf_op jit(solution)/shard_map/ppermute | solution.py:139
  61.5 9.7 %collective-permute-done.2 = bf16[56,2048]{1,0:T(8,128)(2,1)S(1)} collective-permute-done((bf16[56,2048]{1,0:T(8,128)(2,1)S(1)}, bf16[56,2048]{1,0:T(8,128)(2,1)S(1)}, u32[]{:S(2)}, u32[]{:S(2)}) %collective-permute-start.2) | collective-permute-done | bytes 229408 | tf_op jit(solution)/shard_map/ppermute | solution.py:139
  71.4 9.4 %collective-permute-done.9 = bf16[56,2048]{1,0:T(8,128)(2,1)S(1)} collective-permute-done((bf16[56,2048]{1,0:T(8,128)(2,1)S(1)}, bf16[56,2048]{1,0:T(8,128)(2,1)S(1)}, u32[]{:S(2)}, u32[]{:S(2)}) %collective-permute-start.9) | collective-permute-done | bytes 229408 | tf_op jit(solution)/shard_map/ppermute | solution.py:139
  82.4 3.1 collective-permute-done.3
  87.4 2.3 collective-permute-start.13
  89.7 2.7 collective-permute-done.6
  94.0 3.4 %collective-permute-done.13 = bf16[56,2048]{1,0:T(8,128)(2,1)S(1)} collective-permute-done((bf16[56,2048]{1,0:T(8,128)(2,1)S(1)}, bf16[56,2048]{1,0:T(8,128)(2,1)S(1)}, u32[]{:S(2)}, u32[]{:S(2)}) %collective-permute-start.13) | collective-permute-done | bytes 229408 | tf_op jit(solution)/shard_map/ppermute | solution.py:139
  99.0 3.4 %collective-permute-done.7 = bf16[56,2048]{1,0:T(8,128)(2,1)S(1)} collective-permute-done((bf16[56,2048]{1,0:T(8,128)(2,1)S(1)}, bf16[56,2048]{1,0:T(8,128)(2,1)S(1)}, u32[]{:S(2)}, u32[]{:S(2)}) %collective-permute-start.7) | collective-permute-done | bytes 229408 | tf_op jit(solution)/shard_map/ppermute | solution.py:139
  102.4 4.8 %collective-permute-done.14 = bf16[56,2048]{1,0:T(8,128)(2,1)S(1)} collective-permute-done((bf16[56,2048]{1,0:T(8,128)(2,1)S(1)}, bf16[56,2048]{1,0:T(8,128)(2,1)S(1)}, u32[]{:S(2)}, u32[]{:S(2)}) %collective-permute-start.14) | collective-permute-done | bytes 229408 | tf_op jit(solution)/shard_map/ppermute | solution.py:139
  107.3 3.0 subtract_convert_fusion
  111.6 2.0 copy-done.2
  116.5 4.0 %collective-permute-done.15 = bf16[2048,512]{1,0:T(8,128)(2,1)S(1)} collective-permute-done((bf16[2048,512]{1,0:T(8,128)(2,1)}, bf16[2048,512]{1,0:T(8,128)(2,1)S(1)}, u32[]{:S(2)}, u32[]{:S(2)}) %collective-permute-start.15) | collective-permute-done | bytes 2097184 | tf_op jit(solution)/shard_map/ppermute | solution.py:190
  120.5 2.2 fusion.1
  123.8 2.6 collective-permute-start.16
  126.7 2.4 collective-permute-start.18
  129.2 2.8 collective-permute-start.22
  133.0 2.3 collective-permute-start.24
  135.4 3.9 %collective-permute-done.17 = bf16[4,64,512]{2,1,0:T(8,128)(2,1)S(1)} collective-permute-done((bf16[4,64,512]{2,1,0:T(8,128)(2,1)}, bf16[4,64,512]{2,1,0:T(8,128)(2,1)S(1)}, u32[]{:S(2)}, u32[]{:S(2)}) %collective-permute-start.17) | collective-permute-done | bytes 262176 | tf_op jit(solution)/shard_map/ppermute | solution.py:148
  140.4 2.7 collective-permute-start.19
  143.5 2.4 collective-permute-start.21
  146.0 11.1 %collective-permute-start.25 = (bf16[64,512]{1,0:T(8,128)(2,1)S(1)}, bf16[64,512]{1,0:T(8,128)(2,1)S(1)}, u32[]{:S(2)}, u32[]{:S(2)}) collective-permute-start(bf16[64,512]{1,0:T(8,128)(2,1)S(1)} %get-tuple-element.29), channel_id=1, source_target_pairs={{0,8},{1,9},{2,10},{3,11},{4,12},{5,13},{6,14},{7,15},{8,0},{9,1},... | collective-permute-start | bytes 196616 | tf_op jit(solution)/shard_map/ppermute | solution.py:148
  157.2 1.9 collective-permute-start.26
  163.5 4.0 %all-to-all-start = ((bf16[8,16,512]{2,1,0:T(8,128)(2,1)}), bf16[8,16,512]{2,1,0:T(8,128)(2,1)S(1)}, u32[]{:S(2)}, u32[]{:S(2)}) async-start(bf16[8,16,512]{2,1,0:T(8,128)(2,1)} %bitcast.43), calls=%async_computation | async-start | bytes 262144 | tf_op jit(solution)/shard_map/all_to_all | solution.py:199
  167.5 7.9 %all-to-all-done = bf16[8,16,512]{2,1,0:T(8,128)(2,1)S(1)} async-done(((bf16[8,16,512]{2,1,0:T(8,128)(2,1)}), bf16[8,16,512]{2,1,0:T(8,128)(2,1)S(1)}, u32[]{:S(2)}, u32[]{:S(2)}) %all-to-all-start) | async-done | bytes 131104 | tf_op jit(solution)/shard_map/all_to_all | solution.py:199
  175.5 18.2 %all_gather.10 = bf16[128,512]{1,0:T(8,128)(2,1)S(1)} all-gather(bf16[16,512]{1,0:T(8,128)(2,1)S(1)} %reduce_sum.12), channel_id=1, replica_groups={{0,32,64,96,128,160,192,224},{16,48,80,112,144,176,208,240},{1,33,65,97..., dimensions={0}, use_global_device_ids=true | all-gather | bytes 147456 | tf_op jit(solution)/shard_map/all_gather | solution.py:204
  199.3 2.0 collective-permute-start.36
  202.0 2.2 collective-permute-start.33
  209.1 2.0 collective-permute-done.32
  212.7 2.5 collective-permute-done.38
  215.4 14.9 %collective-permute-start.40 = (bf16[2048,512]{1,0:T(8,128)(2,1)S(1)}, bf16[2048,512]{1,0:T(8,128)(2,1)}, u32[]{:S(2)}, u32[]{:S(2)}) collective-permute-start(bf16[2048,512]{1,0:T(8,128)(2,1)S(1)} %bitcast.191), channel_id=1, source_target_pairs={{0,16},{16,0},{32,48},{48,32},{64,80},{80,64},{96,112},{112,96},{1... | collective-permute-start | bytes 6291464 | tf_op jit(solution)/shard_map/ppermute | solution.py:211
  231.5 3.4 %all-to-all-start.1 = ((f32[16,1,3584]{2,1,0:T(1,128)}), f32[16,1,3584]{2,1,0:T(1,128)S(1)}, u32[]{:S(2)}, u32[]{:S(2)}) async-start(f32[16,1,3584]{2,1,0:T(1,128)} %reshape.139), calls=%async_computation.1 | async-start | bytes 458752 | tf_op jit(solution)/shard_map/all_to_all | solution.py:175
  234.9 11.1 %all-to-all-done.1 = f32[16,1,3584]{2,1,0:T(1,128)S(1)} async-done(((f32[16,1,3584]{2,1,0:T(1,128)}), f32[16,1,3584]{2,1,0:T(1,128)S(1)}, u32[]{:S(2)}, u32[]{:S(2)}) %all-to-all-start.1) | async-done | bytes 229408 | tf_op jit(solution)/shard_map/all_to_all | solution.py:175
  248.1 3.2 maximum_select_fusion
  252.1 2.4 fusion.53.gram_ref
  254.5 18.9 %shard_map.75 = f32[512,512]{1,0:T(8,128)S(1)} custom-call(f32[512,512]{1,0:T(8,128)S(1)} %fusion.53.gram_ref), custom_call_target="tpu_custom_call" | custom-call | tf_op jit(solution)/shard_map/pallas_call | solution.py:109
  274.5 2.3 fusion.54
  276.8 1.9 fusion.55
  281.1 17.0 %all_gather.11 = bf16[896,512]{1,0:T(8,128)(2,1)S(1)} all-gather(bf16[56,512]{1,0:T(8,128)(2,1)S(1)} %get-tuple-element.36), channel_id=1, replica_groups=mesh['dp'=16,'rank'=16] {'dp'}, dimensions={0}, use_global_device_ids=true | all-gather | bytes 974848 | tf_op jit(solution)/shard_map/all_gather | solution.py:234
  299.5 5.0 %all-to-all-start.2 = ((f32[16,1,3584]{2,1,0:T(1,128)}), f32[16,1,3584]{2,1,0:T(1,128)S(1)}, u32[]{:S(2)}, u32[]{:S(2)}) async-start(f32[16,1,3584]{2,1,0:T(1,128)} %reshape.141), calls=%async_computation.2 | async-start | bytes 458752 | tf_op jit(solution)/shard_map/all_to_all | solution.py:239
  307.4 8.2 %all-to-all-done.2 = f32[16,1,3584]{2,1,0:T(1,128)S(1)} async-done(((f32[16,1,3584]{2,1,0:T(1,128)}), f32[16,1,3584]{2,1,0:T(1,128)S(1)}, u32[]{:S(2)}, u32[]{:S(2)}) %all-to-all-start.2) | async-done | bytes 229408 | tf_op jit(solution)/shard_map/all_to_all | solution.py:239
  (139 shorter events, 47.7 us)
Async XLA Ops:
  7.2 100.2 %all-gather.2.cloned.1.call-start = ((), (), s32[]{:S(2)}) async-start(), calls=%async_computation.3 | async-start | bytes 4456448 | tf_op jit(solution)/shard_map/all_gather | solution.py:173
  22.2 9.6 %collective-permute-start = (bf16[8,56,4096]{2,1,0:T(8,128)(2,1)}, bf16[8,56,4096]{2,1,0:T(8,128)(2,1)}, u32[]{:S(2)}, u32[]{:S(2)}) collective-permute-start(bf16[8,56,4096]{2,1,0:T(8,128)(2,1)} %dynamic-slice_bitcast_fusion), channel_id=1, source_target_pairs={{0,16},{16,0},{32,48},{48,32},{64,80},{80,64},{96,112},{112,96},{1... | collective-permute-start | bytes 11010056 | tf_op jit(solution)/shard_map/ppermute | solution.py:125
  37.0 14.5 %collective-permute-start.1 = (bf16[56,2048]{1,0:T(8,128)(2,1)S(1)}, bf16[56,2048]{1,0:T(8,128)(2,1)S(1)}, u32[]{:S(2)}, u32[]{:S(2)}) collective-permute-start(bf16[56,2048]{1,0:T(8,128)(2,1)S(1)} %get-tuple-element.12), channel_id=1, source_target_pairs={{0,32},{16,48},{32,64},{48,80},{64,96},{80,112},{96,128},{112,144}... | collective-permute-start | bytes 688136 | tf_op jit(solution)/shard_map/ppermute | solution.py:139
  37.1 45.2 %collective-permute-start.5 = (bf16[56,2048]{1,0:T(8,128)(2,1)S(1)}, bf16[56,2048]{1,0:T(8,128)(2,1)S(1)}, u32[]{:S(2)}, u32[]{:S(2)}) collective-permute-start(bf16[56,2048]{1,0:T(8,128)(2,1)S(1)} %get-tuple-element.13), channel_id=1, source_target_pairs={{0,224},{16,240},{32,0},{48,16},{64,32},{80,48},{96,64},{112,80},{... | collective-permute-start | bytes 688136 | tf_op jit(solution)/shard_map/ppermute | solution.py:139
  41.1 20.3 %collective-permute-start.8 = (bf16[56,2048]{1,0:T(8,128)(2,1)S(1)}, bf16[56,2048]{1,0:T(8,128)(2,1)S(1)}, u32[]{:S(2)}, u32[]{:S(2)}) collective-permute-start(bf16[56,2048]{1,0:T(8,128)(2,1)S(1)} %get-tuple-element.16), channel_id=1, source_target_pairs={{0,32},{16,48},{32,64},{48,80},{64,96},{80,112},{96,128},{112,144}... | collective-permute-start | bytes 688136 | tf_op jit(solution)/shard_map/ppermute | solution.py:139
  41.2 30.2 %collective-permute-start.11 = (bf16[56,2048]{1,0:T(8,128)(2,1)S(1)}, bf16[56,2048]{1,0:T(8,128)(2,1)S(1)}, u32[]{:S(2)}, u32[]{:S(2)}) collective-permute-start(bf16[56,2048]{1,0:T(8,128)(2,1)S(1)} %get-tuple-element.17), channel_id=1, source_target_pairs={{0,224},{16,240},{32,0},{48,16},{64,32},{80,48},{96,64},{112,80},{... | collective-permute-start | bytes 688136 | tf_op jit(solution)/shard_map/ppermute | solution.py:139
  51.6 19.6 %collective-permute-start.2 = (bf16[56,2048]{1,0:T(8,128)(2,1)S(1)}, bf16[56,2048]{1,0:T(8,128)(2,1)S(1)}, u32[]{:S(2)}, u32[]{:S(2)}) collective-permute-start(bf16[56,2048]{1,0:T(8,128)(2,1)S(1)} %fusion.27), channel_id=1, source_target_pairs={{0,32},{16,48},{32,64},{48,80},{64,96},{80,112},{96,128},{112,144}... | collective-permute-start | bytes 688136 | tf_op jit(solution)/shard_map/ppermute | solution.py:139
  61.4 19.3 %collective-permute-start.9 = (bf16[56,2048]{1,0:T(8,128)(2,1)S(1)}, bf16[56,2048]{1,0:T(8,128)(2,1)S(1)}, u32[]{:S(2)}, u32[]{:S(2)}) collective-permute-start(bf16[56,2048]{1,0:T(8,128)(2,1)S(1)} %fusion.21), channel_id=1, source_target_pairs={{0,32},{16,48},{32,64},{48,80},{64,96},{80,112},{96,128},{112,144}... | collective-permute-start | bytes 688136 | tf_op jit(solution)/shard_map/ppermute | solution.py:139
  71.3 14.3 %collective-permute-start.3 = (bf16[56,2048]{1,0:T(8,128)(2,1)S(1)}, bf16[56,2048]{1,0:T(8,128)(2,1)S(1)}, u32[]{:S(2)}, u32[]{:S(2)}) collective-permute-start(bf16[56,2048]{1,0:T(8,128)(2,1)S(1)} %fusion.28), channel_id=1, source_target_pairs={{0,32},{16,48},{32,64},{48,80},{64,96},{80,112},{96,128},{112,144}... | collective-permute-start | bytes 688136 | tf_op jit(solution)/shard_map/ppermute | solution.py:139
  80.8 6.5 %collective-permute-start.12 = (bf16[56,2048]{1,0:T(8,128)(2,1)S(1)}, bf16[56,2048]{1,0:T(8,128)(2,1)S(1)}, u32[]{:S(2)}, u32[]{:S(2)}) collective-permute-start(bf16[56,2048]{1,0:T(8,128)(2,1)S(1)} %get-tuple-element.15), channel_id=1, source_target_pairs={{0,224},{16,240},{32,0},{48,16},{64,32},{80,48},{96,64},{112,80},{... | collective-permute-start | bytes 688136 | tf_op jit(solution)/shard_map/ppermute | solution.py:139
  81.7 20.7 %collective-permute-start.10 = (bf16[56,2048]{1,0:T(8,128)(2,1)S(1)}, bf16[56,2048]{1,0:T(8,128)(2,1)S(1)}, u32[]{:S(2)}, u32[]{:S(2)}) collective-permute-start(bf16[56,2048]{1,0:T(8,128)(2,1)S(1)} %get-tuple-element.14), channel_id=1, source_target_pairs={{0,32},{16,48},{32,64},{48,80},{64,96},{80,112},{96,128},{112,144}... | collective-permute-start | bytes 688136 | tf_op jit(solution)/shard_map/ppermute | solution.py:139
  85.6 6.8 %collective-permute-start.6 = (bf16[56,2048]{1,0:T(8,128)(2,1)S(1)}, bf16[56,2048]{1,0:T(8,128)(2,1)S(1)}, u32[]{:S(2)}, u32[]{:S(2)}) collective-permute-start(bf16[56,2048]{1,0:T(8,128)(2,1)S(1)} %get-tuple-element.11), channel_id=1, source_target_pairs={{0,224},{16,240},{32,0},{48,16},{64,32},{80,48},{96,64},{112,80},{... | collective-permute-start | bytes 688136 | tf_op jit(solution)/shard_map/ppermute | solution.py:139
  86.7 12.3 %collective-permute-start.4 = (bf16[56,2048]{1,0:T(8,128)(2,1)S(1)}, bf16[56,2048]{1,0:T(8,128)(2,1)S(1)}, u32[]{:S(2)}, u32[]{:S(2)}) collective-permute-start(bf16[56,2048]{1,0:T(8,128)(2,1)S(1)} %get-tuple-element.10), channel_id=1, source_target_pairs={{0,32},{16,48},{32,64},{48,80},{64,96},{80,112},{96,128},{112,144}... | collective-permute-start | bytes 688136 | tf_op jit(solution)/shard_map/ppermute | solution.py:139
  87.4 10.0 %collective-permute-start.13 = (bf16[56,2048]{1,0:T(8,128)(2,1)S(1)}, bf16[56,2048]{1,0:T(8,128)(2,1)S(1)}, u32[]{:S(2)}, u32[]{:S(2)}) collective-permute-start(bf16[56,2048]{1,0:T(8,128)(2,1)S(1)} %fusion.19), channel_id=1, source_target_pairs={{0,224},{16,240},{32,0},{48,16},{64,32},{80,48},{96,64},{112,80},{... | collective-permute-start | bytes 688136 | tf_op jit(solution)/shard_map/ppermute | solution.py:139
  92.5 9.8 %collective-permute-start.7 = (bf16[56,2048]{1,0:T(8,128)(2,1)S(1)}, bf16[56,2048]{1,0:T(8,128)(2,1)S(1)}, u32[]{:S(2)}, u32[]{:S(2)}) collective-permute-start(bf16[56,2048]{1,0:T(8,128)(2,1)S(1)} %fusion.26), channel_id=1, source_target_pairs={{0,224},{16,240},{32,0},{48,16},{64,32},{80,48},{96,64},{112,80},{... | collective-permute-start | bytes 688136 | tf_op jit(solution)/shard_map/ppermute | solution.py:139
  97.5 9.8 %collective-permute-start.14 = (bf16[56,2048]{1,0:T(8,128)(2,1)S(1)}, bf16[56,2048]{1,0:T(8,128)(2,1)S(1)}, u32[]{:S(2)}, u32[]{:S(2)}) collective-permute-start(bf16[56,2048]{1,0:T(8,128)(2,1)S(1)} %fusion.20), channel_id=1, source_target_pairs={{0,224},{16,240},{32,0},{48,16},{64,32},{80,48},{96,64},{112,80},{... | collective-permute-start | bytes 688136 | tf_op jit(solution)/shard_map/ppermute | solution.py:139
  115.1 5.4 %collective-permute-start.15 = (bf16[2048,512]{1,0:T(8,128)(2,1)}, bf16[2048,512]{1,0:T(8,128)(2,1)S(1)}, u32[]{:S(2)}, u32[]{:S(2)}) collective-permute-start(bf16[2048,512]{1,0:T(8,128)(2,1)} %dynamic-slice_bitcast_fusion.1), channel_id=1, source_target_pairs={{0,16},{16,0},{32,48},{48,32},{64,80},{80,64},{96,112},{112,96},{1... | collective-permute-start | bytes 6291464 | tf_op jit(solution)/shard_map/ppermute | solution.py:190
  123.8 9.3 %collective-permute-start.16 = (bf16[4,64,512]{2,1,0:T(8,128)(2,1)}, bf16[4,64,512]{2,1,0:T(8,128)(2,1)S(1)}, u32[]{:S(2)}, u32[]{:S(2)}) collective-permute-start(bf16[4,64,512]{2,1,0:T(8,128)(2,1)} %get-tuple-element.18), channel_id=1, source_target_pairs={{0,8},{1,9},{2,10},{3,11},{4,12},{5,13},{6,14},{7,15},{8,0},{9,1},... | collective-permute-start | bytes 786440 | tf_op jit(solution)/shard_map/ppermute | solution.py:148
  126.4 12.9 %collective-permute-start.17 = (bf16[4,64,512]{2,1,0:T(8,128)(2,1)}, bf16[4,64,512]{2,1,0:T(8,128)(2,1)S(1)}, u32[]{:S(2)}, u32[]{:S(2)}) collective-permute-start(bf16[4,64,512]{2,1,0:T(8,128)(2,1)} %get-tuple-element.19), channel_id=1, source_target_pairs={{0,4},{1,5},{2,6},{3,7},{4,8},{5,9},{6,10},{7,11},{8,12},{9,13},{1... | collective-permute-start | bytes 786440 | tf_op jit(solution)/shard_map/ppermute | solution.py:148
  126.7 12.7 %collective-permute-start.18 = (bf16[4,64,512]{2,1,0:T(8,128)(2,1)S(1)}, bf16[4,64,512]{2,1,0:T(8,128)(2,1)}, u32[]{:S(2)}, u32[]{:S(2)}) collective-permute-start(bf16[4,64,512]{2,1,0:T(8,128)(2,1)S(1)} %get-tuple-element.20), channel_id=1, source_target_pairs={{0,12},{1,13},{2,14},{3,15},{4,0},{5,1},{6,2},{7,3},{8,4},{9,5},{1... | collective-permute-start | bytes 786440 | tf_op jit(solution)/shard_map/ppermute | solution.py:148
  129.2 14.3 %collective-permute-start.22 = (bf16[4,64,512]{2,1,0:T(8,128)(2,1)S(1)}, bf16[4,64,512]{2,1,0:T(8,128)(2,1)S(1)}, u32[]{:S(2)}, u32[]{:S(2)}) collective-permute-start(bf16[4,64,512]{2,1,0:T(8,128)(2,1)S(1)} %get-tuple-element.21), channel_id=1, source_target_pairs={{0,2},{1,3},{2,0},{3,1},{4,6},{5,7},{6,4},{7,5},{8,10},{9,11},{10,... | collective-permute-start | bytes 786440 | tf_op jit(solution)/shard_map/ppermute | solution.py:148
  131.9 13.9 %collective-permute-start.23 = (bf16[4,64,512]{2,1,0:T(8,128)(2,1)S(1)}, bf16[4,64,512]{2,1,0:T(8,128)(2,1)S(1)}, u32[]{:S(2)}, u32[]{:S(2)}) collective-permute-start(bf16[4,64,512]{2,1,0:T(8,128)(2,1)S(1)} %get-tuple-element.23), channel_id=1, source_target_pairs={{0,1},{1,2},{2,3},{3,0},{4,5},{5,6},{6,7},{7,4},{8,9},{9,10},{10,1... | collective-permute-start | bytes 786440 | tf_op jit(solution)/shard_map/ppermute | solution.py:148
  133.0 12.8 %collective-permute-start.24 = (bf16[4,64,512]{2,1,0:T(8,128)(2,1)S(1)}, bf16[4,64,512]{2,1,0:T(8,128)(2,1)S(1)}, u32[]{:S(2)}, u32[]{:S(2)}) collective-permute-start(bf16[4,64,512]{2,1,0:T(8,128)(2,1)S(1)} %get-tuple-element.22), channel_id=1, source_target_pairs={{0,3},{1,0},{2,1},{3,2},{4,7},{5,4},{6,5},{7,6},{8,11},{9,8},{10,9... | collective-permute-start | bytes 786440 | tf_op jit(solution)/shard_map/ppermute | solution.py:148
  140.4 18.6 %collective-permute-start.19 = (bf16[64,512]{1,0:T(8,128)(2,1)S(1)}, bf16[64,512]{1,0:T(8,128)(2,1)S(1)}, u32[]{:S(2)}, u32[]{:S(2)}) collective-permute-start(bf16[64,512]{1,0:T(8,128)(2,1)S(1)} %get-tuple-element.26), channel_id=1, source_target_pairs={{0,2},{1,3},{2,0},{3,1},{4,6},{5,7},{6,4},{7,5},{8,10},{9,11},{10,... | collective-permute-start | bytes 196616 | tf_op jit(solution)/shard_map/ppermute | solution.py:148
  143.2 16.7 %collective-permute-start.20 = (bf16[64,512]{1,0:T(8,128)(2,1)S(1)}, bf16[64,512]{1,0:T(8,128)(2,1)S(1)}, u32[]{:S(2)}, u32[]{:S(2)}) collective-permute-start(bf16[64,512]{1,0:T(8,128)(2,1)S(1)} %get-tuple-element.28), channel_id=1, source_target_pairs={{0,1},{1,2},{2,3},{3,0},{4,5},{5,6},{6,7},{7,4},{8,9},{9,10},{10,1... | collective-permute-start | bytes 196616 | tf_op jit(solution)/shard_map/ppermute | solution.py:148
  143.5 16.4 %collective-permute-start.21 = (bf16[64,512]{1,0:T(8,128)(2,1)S(1)}, bf16[64,512]{1,0:T(8,128)(2,1)S(1)}, u32[]{:S(2)}, u32[]{:S(2)}) collective-permute-start(bf16[64,512]{1,0:T(8,128)(2,1)S(1)} %get-tuple-element.27), channel_id=1, source_target_pairs={{0,3},{1,0},{2,1},{3,2},{4,7},{5,4},{6,5},{7,6},{8,11},{9,8},{10,9... | collective-permute-start | bytes 196616 | tf_op jit(solution)/shard_map/ppermute | solution.py:148
  146.0 14.5 %collective-permute-start.25 = (bf16[64,512]{1,0:T(8,128)(2,1)S(1)}, bf16[64,512]{1,0:T(8,128)(2,1)S(1)}, u32[]{:S(2)}, u32[]{:S(2)}) collective-permute-start(bf16[64,512]{1,0:T(8,128)(2,1)S(1)} %get-tuple-element.29), channel_id=1, source_target_pairs={{0,8},{1,9},{2,10},{3,11},{4,12},{5,13},{6,14},{7,15},{8,0},{9,1},... | collective-permute-start | bytes 196616 | tf_op jit(solution)/shard_map/ppermute | solution.py:148
  157.2 4.3 %collective-permute-start.26 = (bf16[64,512]{1,0:T(8,128)(2,1)S(1)}, bf16[64,512]{1,0:T(8,128)(2,1)S(1)}, u32[]{:S(2)}, u32[]{:S(2)}) collective-permute-start(bf16[64,512]{1,0:T(8,128)(2,1)S(1)} %get-tuple-element.31), channel_id=1, source_target_pairs={{0,4},{1,5},{2,6},{3,7},{4,8},{5,9},{6,10},{7,11},{8,12},{9,13},{1... | collective-permute-start | bytes 196616 | tf_op jit(solution)/shard_map/ppermute | solution.py:148
  159.0 3.8 %collective-permute-start.27 = (bf16[64,512]{1,0:T(8,128)(2,1)S(1)}, bf16[64,512]{1,0:T(8,128)(2,1)S(1)}, u32[]{:S(2)}, u32[]{:S(2)}) collective-permute-start(bf16[64,512]{1,0:T(8,128)(2,1)S(1)} %get-tuple-element.30), channel_id=1, source_target_pairs={{0,12},{1,13},{2,14},{3,15},{4,0},{5,1},{6,2},{7,3},{8,4},{9,5},{1... | collective-permute-start | bytes 196616 | tf_op jit(solution)/shard_map/ppermute | solution.py:148
  163.5 11.9 %all-to-all-start = ((bf16[8,16,512]{2,1,0:T(8,128)(2,1)}), bf16[8,16,512]{2,1,0:T(8,128)(2,1)S(1)}, u32[]{:S(2)}, u32[]{:S(2)}) async-start(bf16[8,16,512]{2,1,0:T(8,128)(2,1)} %bitcast.43), calls=%async_computation | async-start | bytes 262144 | tf_op jit(solution)/shard_map/all_to_all | solution.py:199
  193.7 5.6 %collective-permute-start.28 = (bf16[64,512]{1,0:T(8,128)(2,1)S(1)}, bf16[64,512]{1,0:T(8,128)(2,1)S(1)}, u32[]{:S(2)}, u32[]{:S(2)}) collective-permute-start(bf16[64,512]{1,0:T(8,128)(2,1)S(1)} %get-tuple-element.34), channel_id=1, source_target_pairs={{0,2},{1,3},{2,0},{3,1},{4,6},{5,7},{6,4},{7,5},{8,10},{9,11},{10,... | collective-permute-start | bytes 196616 | tf_op jit(solution)/shard_map/ppermute | solution.py:157
  194.0 7.3 %collective-permute-start.29 = (bf16[64,512]{1,0:T(8,128)(2,1)S(1)}, bf16[64,512]{1,0:T(8,128)(2,1)S(1)}, u32[]{:S(2)}, u32[]{:S(2)}) collective-permute-start(bf16[64,512]{1,0:T(8,128)(2,1)S(1)} %get-tuple-element.34), channel_id=1, source_target_pairs={{0,1},{1,2},{2,3},{3,0},{4,5},{5,6},{6,7},{7,4},{8,9},{9,10},{10,1... | collective-permute-start | bytes 196616 | tf_op jit(solution)/shard_map/ppermute | solution.py:157
  195.0 6.3 %collective-permute-start.30 = (bf16[64,512]{1,0:T(8,128)(2,1)S(1)}, bf16[64,512]{1,0:T(8,128)(2,1)S(1)}, u32[]{:S(2)}, u32[]{:S(2)}) collective-permute-start(bf16[64,512]{1,0:T(8,128)(2,1)S(1)} %get-tuple-element.34), channel_id=1, source_target_pairs={{0,3},{1,0},{2,1},{3,2},{4,7},{5,4},{6,5},{7,6},{8,11},{9,8},{10,9... | collective-permute-start | bytes 196616 | tf_op jit(solution)/shard_map/ppermute | solution.py:157
  196.7 5.4 %collective-permute-start.34 = (bf16[64,512]{1,0:T(8,128)(2,1)S(1)}, bf16[64,512]{1,0:T(8,128)(2,1)S(1)}, u32[]{:S(2)}, u32[]{:S(2)}) collective-permute-start(bf16[64,512]{1,0:T(8,128)(2,1)S(1)} %get-tuple-element.35), channel_id=1, source_target_pairs={{0,8},{1,9},{2,10},{3,11},{4,12},{5,13},{6,14},{7,15},{8,0},{9,1},... | collective-permute-start | bytes 196616 | tf_op jit(solution)/shard_map/ppermute | solution.py:157
  198.4 5.8 %collective-permute-start.35 = (bf16[64,512]{1,0:T(8,128)(2,1)S(1)}, bf16[64,512]{1,0:T(8,128)(2,1)S(1)}, u32[]{:S(2)}, u32[]{:S(2)}) collective-permute-start(bf16[64,512]{1,0:T(8,128)(2,1)S(1)} %get-tuple-element.35), channel_id=1, source_target_pairs={{0,4},{1,5},{2,6},{3,7},{4,8},{5,9},{6,10},{7,11},{8,12},{9,13},{1... | collective-permute-start | bytes 196616 | tf_op jit(solution)/shard_map/ppermute | solution.py:157
  199.3 5.0 %collective-permute-start.36 = (bf16[64,512]{1,0:T(8,128)(2,1)S(1)}, bf16[64,512]{1,0:T(8,128)(2,1)S(1)}, u32[]{:S(2)}, u32[]{:S(2)}) collective-permute-start(bf16[64,512]{1,0:T(8,128)(2,1)S(1)} %get-tuple-element.35), channel_id=1, source_target_pairs={{0,12},{1,13},{2,14},{3,15},{4,0},{5,1},{6,2},{7,3},{8,4},{9,5},{1... | collective-permute-start | bytes 196616 | tf_op jit(solution)/shard_map/ppermute | solution.py:157
  201.3 6.9 %collective-permute-start.31 = (bf16[4,64,512]{2,1,0:T(8,128)(2,1)S(1)}, bf16[4,64,512]{2,1,0:T(8,128)(2,1)S(1)}, u32[]{:S(2)}, u32[]{:S(2)}) collective-permute-start(bf16[4,64,512]{2,1,0:T(8,128)(2,1)S(1)} %bitcast_dynamic-update-slice_fusion.12), channel_id=1, source_target_pairs={{0,8},{1,9},{2,10},{3,11},{4,12},{5,13},{6,14},{7,15},{8,0},{9,1},... | collective-permute-start | bytes 786440 | tf_op jit(solution)/shard_map/ppermute | solution.py:157
  201.4 9.6 %collective-permute-start.32 = (bf16[4,64,512]{2,1,0:T(8,128)(2,1)S(1)}, bf16[4,64,512]{2,1,0:T(8,128)(2,1)S(1)}, u32[]{:S(2)}, u32[]{:S(2)}) collective-permute-start(bf16[4,64,512]{2,1,0:T(8,128)(2,1)S(1)} %bitcast_dynamic-update-slice_fusion.12), channel_id=1, source_target_pairs={{0,4},{1,5},{2,6},{3,7},{4,8},{5,9},{6,10},{7,11},{8,12},{9,13},{1... | collective-permute-start | bytes 786440 | tf_op jit(solution)/shard_map/ppermute | solution.py:157
  202.0 9.1 %collective-permute-start.33 = (bf16[4,64,512]{2,1,0:T(8,128)(2,1)S(1)}, bf16[4,64,512]{2,1,0:T(8,128)(2,1)S(1)}, u32[]{:S(2)}, u32[]{:S(2)}) collective-permute-start(bf16[4,64,512]{2,1,0:T(8,128)(2,1)S(1)} %bitcast_dynamic-update-slice_fusion.12), channel_id=1, source_target_pairs={{0,12},{1,13},{2,14},{3,15},{4,0},{5,1},{6,2},{7,3},{8,4},{9,5},{1... | collective-permute-start | bytes 786440 | tf_op jit(solution)/shard_map/ppermute | solution.py:157
  204.3 8.4 %collective-permute-start.37 = (bf16[4,64,512]{2,1,0:T(8,128)(2,1)S(1)}, bf16[4,64,512]{2,1,0:T(8,128)(2,1)S(1)}, u32[]{:S(2)}, u32[]{:S(2)}) collective-permute-start(bf16[4,64,512]{2,1,0:T(8,128)(2,1)S(1)} %bitcast_dynamic-update-slice_fusion.8), channel_id=1, source_target_pairs={{0,2},{1,3},{2,0},{3,1},{4,6},{5,7},{6,4},{7,5},{8,10},{9,11},{10,... | collective-permute-start | bytes 786440 | tf_op jit(solution)/shard_map/ppermute | solution.py:157
  206.0 9.2 %collective-permute-start.38 = (bf16[4,64,512]{2,1,0:T(8,128)(2,1)S(1)}, bf16[4,64,512]{2,1,0:T(8,128)(2,1)S(1)}, u32[]{:S(2)}, u32[]{:S(2)}) collective-permute-start(bf16[4,64,512]{2,1,0:T(8,128)(2,1)S(1)} %bitcast_dynamic-update-slice_fusion.8), channel_id=1, source_target_pairs={{0,1},{1,2},{2,3},{3,0},{4,5},{5,6},{6,7},{7,4},{8,9},{9,10},{10,1... | collective-permute-start | bytes 786440 | tf_op jit(solution)/shard_map/ppermute | solution.py:157
  206.5 23.8 %copy-start.4 = (f32[32,896]{1,0:T(8,128)S(1)}, f32[32,896]{1,0:T(8,128)}, u32[]{:S(2)}) copy-start(f32[32,896]{1,0:T(8,128)} %param.7) | copy-start | bytes 344068
  206.5 23.8 %copy-start.5 = (f32[32,896]{1,0:T(8,128)S(1)}, f32[32,896]{1,0:T(8,128)}, u32[]{:S(2)}) copy-start(f32[32,896]{1,0:T(8,128)} %param.6) | copy-start | bytes 344068
  208.3 6.9 %collective-permute-start.39 = (bf16[4,64,512]{2,1,0:T(8,128)(2,1)S(1)}, bf16[4,64,512]{2,1,0:T(8,128)(2,1)S(1)}, u32[]{:S(2)}, u32[]{:S(2)}) collective-permute-start(bf16[4,64,512]{2,1,0:T(8,128)(2,1)S(1)} %bitcast_dynamic-update-slice_fusion.8), channel_id=1, source_target_pairs={{0,3},{1,0},{2,1},{3,2},{4,7},{5,4},{6,5},{7,6},{8,11},{9,8},{10,9... | collective-permute-start | bytes 786440 | tf_op jit(solution)/shard_map/ppermute | solution.py:157
  215.4 32.6 %collective-permute-start.40 = (bf16[2048,512]{1,0:T(8,128)(2,1)S(1)}, bf16[2048,512]{1,0:T(8,128)(2,1)}, u32[]{:S(2)}, u32[]{:S(2)}) collective-permute-start(bf16[2048,512]{1,0:T(8,128)(2,1)S(1)} %bitcast.191), channel_id=1, source_target_pairs={{0,16},{16,0},{32,48},{48,32},{64,80},{80,64},{96,112},{112,96},{1... | collective-permute-start | bytes 6291464 | tf_op jit(solution)/shard_map/ppermute | solution.py:211
  231.5 14.5 %all-to-all-start.1 = ((f32[16,1,3584]{2,1,0:T(1,128)}), f32[16,1,3584]{2,1,0:T(1,128)S(1)}, u32[]{:S(2)}, u32[]{:S(2)}) async-start(f32[16,1,3584]{2,1,0:T(1,128)} %reshape.139), calls=%async_computation.1 | async-start | bytes 458752 | tf_op jit(solution)/shard_map/all_to_all | solution.py:175
  251.3 23.1 %copy-start = (bf16[4096,512]{1,0:T(8,128)(2,1)}, bf16[4096,512]{1,0:T(8,128)(2,1)S(1)}, u32[]{:S(2)}) copy-start(bf16[4096,512]{1,0:T(8,128)(2,1)S(1)} %maximum_select_fusion) | copy-start | bytes 12582916
  299.5 16.0 %all-to-all-start.2 = ((f32[16,1,3584]{2,1,0:T(1,128)}), f32[16,1,3584]{2,1,0:T(1,128)S(1)}, u32[]{:S(2)}, u32[]{:S(2)}) async-start(f32[16,1,3584]{2,1,0:T(1,128)} %reshape.141), calls=%async_computation.2 | async-start | bytes 458752 | tf_op jit(solution)/shard_map/all_to_all | solution.py:239
  (3 other events, 36.0 us)
Sparse Core Ops, SparseCore 0:
  25.6 56.6 all-gather.1
